TPU v7x, 256 devices: a whole 4x4x8 slice. The times are simulated.
256 devices in a mesh: dp: 64 (over z_hi, x, y, core), mp: 4 (over z_lo).
Axes of the slice: x: 4, y: 4, z: 8 (z_hi: 2, z_lo: 4; z = z_hi * 4 + z_lo), core: 2. Of those that a mesh axis runs over, the one named last changes fastest.
Arguments:
- activations: bfloat16 [49152, 4096], P('dp', 'mp'), may hold values from -16 to 16
- out_grads: bfloat16 [49152, 4096], P('dp', 'mp'), may hold values from -0.125 to 0.125
- weight: float32 [4096, 4096], P('dp', 'mp'), may hold values from -0.09375 to 0.09375
- row_moment: float32 [4096], P('dp'), may hold values from 0.05 to 2
- col_moment: float32 [4096], P('mp'), may hold values from 0.05 to 2
Outputs:
- new_weight: float32 [4096, 4096], P('dp', 'mp')
- update: float32 [4096, 4096], P('dp', 'mp')
- new_row: float32 [4096], P('dp')
- new_col: float32 [4096], P('mp')
All inputs are finite; a program needn't handle non-finite values.
Results may differ from a plain program's by a relative error of at most 0.0003.
Values may be sent and summed in bfloat16 or wider, within the bound.
A program may use at most 64 MiB of HBM per device.

v0:
```python
import jax
import jax.numpy as jnp
from jax import lax
from jax.sharding import PartitionSpec as P

D = 4096
STEPS_DONE = 10


learn_rate = 0.01
tiny_eps = 1e-30


def body(activations, out_grads, weight, row_moment, col_moment):
    partial_grad = lax.dot_general(
        lax.all_gather(activations, "mp", axis=1, tiled=True),
        out_grads,
        (((0,), (0,)), ((), ())),
        preferred_element_type=jnp.float32,
    )
    gradient = lax.psum_scatter(partial_grad, "dp", scatter_dimension=0, tiled=True)
    decay = 1.0 - STEPS_DONE ** (-0.8)
    squared = gradient * gradient + tiny_eps
    row_total_sq = lax.psum(jnp.sum(squared, axis=1), "mp")
    new_row = decay * row_moment + (1.0 - decay) * (row_total_sq / D)
    col_part, row_total = lax.psum((jnp.sum(squared, axis=0), jnp.sum(new_row)), "dp")
    new_col = decay * col_moment + (1.0 - decay) * (col_part / D)
    scale_total = row_total / D
    scaled = gradient / jnp.sqrt(new_row[:, None] * new_col[None, :] / scale_total)
    clip_sum = lax.psum(jnp.sum(scaled * scaled), ("dp", "mp"))
    root_mean = jnp.sqrt(clip_sum / (D * D))
    update = scaled / jnp.maximum(1.0, root_mean)
    new_weight = weight - learn_rate * update
    return (new_weight, update, new_row, new_col)


def solution(mesh):
    return jax.shard_map(
        body,
        mesh=mesh,
        in_specs=(P("dp", "mp"), P("dp", "mp"), P("dp", "mp"), P("dp"), P("mp")),
        out_specs=(P("dp", "mp"), P("dp", "mp"), P("dp"), P("mp")),
        check_vma=False,
    )
```

profile of v0, /device:TPU:1, one launch (start us, length us, event | category | flops | bytes accessed | tf_op | source)
XLA Modules:
  0.0 886.2 jit_solution(465518559793790597)
XLA Ops:
  7.2 0.0 copy-start
  7.2 0.0 all-gather.2.cloned.1.call-start
  7.2 0.7 all-gather.2.cloned.1.call-update
  7.9 0.0 reduce-scatter.2.cloned.1.call-start
  8.0 124.2 %all-gather.2.cloned.1.call-done = bf16[768,4096]{1,0:T(8,128)(2,1)} async-done(((bf16[768,1024]{1,0:T(8,128)(2,1)}), bf16[768,4096]{1,0:T(8,128)(2,1)}) %all-gather.2.cloned.1.call-update) | async-done | bytes 6291472 | tf_op jit(solution)/shard_map/all_gather | solution.py:16
  132.2 0.0 copy-done
  132.2 13.0 %fusion.3 = f32[4096,1024]{1,0:T(8,128)} fusion(bf16[768,4096]{1,0:T(8,128)(2,1)} %all-gather.2.cloned.1.call-done, bf16[768,1024]{1,0:T(8,128)(2,1)S(1)} %copy-done), kind=kOutput, calls=%fused_computation.10 | convolution fusion | flops 6442450944 | bytes 24641536 | tf_op jit(solution)/shard_map/dot_general | solution.py:15
  145.2 0.0 copy-start.5
  145.2 0.0 copy-start.4
  145.2 0.0 copy-start.1
  145.2 0.0 reduce-scatter.2.cloned.1.call-update
  145.3 432.3 %reduce-scatter.2.cloned.1.call-done = f32[64,1024]{1,0:T(8,128)} async-done(((f32[4096,1024]{1,0:T(8,128)}), f32[64,1024]{1,0:T(8,128)}) %reduce-scatter.2.cloned.1.call-update) | async-done | bytes 262160 | tf_op jit(solution)/shard_map/reduce_scatter | solution.py:21
  577.5 1.1 fusion
  578.6 8.9 %psum.28 = f32[64]{0:T(128)S(1)} all-reduce(f32[64]{0:T(128)S(1)} %get-tuple-element.5), channel_id=1, replica_groups=mesh['dp'=64,'mp'=4] {'mp'}, use_global_device_ids=true, to_apply=%region_2.0 | all-reduce | flops 64 | bytes 512 | tf_op jit(solution)/shard_map/psum | solution.py:24
  587.6 0.0 copy-done.5
  587.6 0.6 fusion.2
  588.2 0.0 copy-start.3
  588.2 213.8 %all-reduce = (f32[]{:T(128)}, f32[1024]{0:T(1024)S(1)}) all-reduce(f32[]{:T(128)} %get-tuple-element.10, f32[1024]{0:T(1024)S(1)} %get-tuple-element.4), channel_id=1, replica_groups=mesh['dp'=64,'mp'=4] {'dp'}, use_global_device_ids=true, to_apply=%region_6.0 | all-reduce | flops 1025 | bytes 8200 | tf_op jit(solution)/shard_map/psum | solution.py:26
  802.6 0.0 copy-done.4
  802.6 0.0 copy-start.2
  802.6 1.7 multiply_reduce_fusion
  804.3 72.4 %psum.31 = f32[]{:T(128)} all-reduce(f32[]{:T(128)} %multiply_reduce_fusion), channel_id=1, replica_groups=mesh['dp'=64,'mp'=4] {'dp','mp'}, use_global_device_ids=true, to_apply=%region_8.0 | all-reduce | flops 1 | bytes 8 | tf_op jit(solution)/shard_map/psum | solution.py:30
  877.4 0.0 copy-done.1
  877.4 1.9 multiply_subtract_fusion
  879.3 0.0 copy-done.3
  879.3 0.0 copy-done.2
  (1 shorter events, 0.0 us)
Async XLA Ops:
  7.2 125.0 %copy-start = (bf16[768,1024]{1,0:T(8,128)(2,1)S(1)}, bf16[768,1024]{1,0:T(8,128)(2,1)}, u32[]{:S(2)}) copy-start(bf16[768,1024]{1,0:T(8,128)(2,1)} %param.6) | copy-start | bytes 4718596
  7.2 125.0 %all-gather.2.cloned.1.call-start = ((), (), s32[]{:S(2)}) async-start(), calls=%async_computation.1 | async-start | bytes 7864320 | tf_op jit(solution)/shard_map/all_gather | solution.py:16
  7.9 569.6 %reduce-scatter.2.cloned.1.call-start = ((), (), s32[]{:S(2)}) async-start(), calls=%async_computation.2 | async-start | bytes 17039360 | tf_op jit(solution)/shard_map/reduce_scatter | solution.py:21
  145.2 442.3 %copy-start.5 = (f32[64]{0:T(128)S(1)}, f32[64]{0:T(128)}, u32[]{:S(2)}) copy-start(f32[64]{0:T(128)} %param.8) | copy-start | bytes 772
  145.2 657.4 %copy-start.4 = (f32[1024]{0:T(1024)S(1)}, f32[1024]{0:T(1024)}, u32[]{:S(2)}) copy-start(f32[1024]{0:T(1024)} %param.9) | copy-start | bytes 12292
  145.2 732.2 %copy-start.1 = (f32[64,1024]{1,0:T(8,128)S(1)}, f32[64,1024]{1,0:T(8,128)}, u32[]{:S(2)}) copy-start(f32[64,1024]{1,0:T(8,128)} %param.7) | copy-start | bytes 786436
  588.2 291.1 %copy-start.3 = (f32[64]{0:T(128)}, f32[64]{0:T(128)S(1)}, u32[]{:S(2)}) copy-start(f32[64]{0:T(128)S(1)} %get-tuple-element.11) | copy-start | bytes 772
  802.6 76.7 %copy-start.2 = (f32[1024]{0:T(1024)}, f32[1024]{0:T(1024)S(1)}, u32[]{:S(2)}) copy-start(f32[1024]{0:T(1024)S(1)} %multiply_add_fusion.1) | copy-start | bytes 12292
Sparse Core Ops, SparseCore 0:
  9.8 122.3 all-gather.1
  145.4 432.1 reduce-scatter.1
where the time goes:
time: 886 us
  waiting for transfers between devices  557 us (63%)
  blocking collectives  295 us (33%)
  between operations  15.4 us (2%)
  matrix products  13 us (1%)
    reduce_scatter x1, waiting for transfers between devices, body(): lax.psum_scatter(partial_grad, 'dp', scatter_dimension=0, tiled=True)  432 us
    psum x1, blocking collectives, body(): lax.psum((jnp.sum(squared, axis=0), jnp.sum(new_row)), 'dp')  214 us
    all_gather x1, waiting for transfers between devices, body(): lax.all_gather(activations, 'mp', axis=1, tiled=True)  124 us
    psum x1, blocking collectives, body(): clip_sum = lax.psum(jnp.sum(scaled * scaled), ('dp', 'mp'))  72.4 us
  transfers between devices with their start and end apart: 2, of which 2 were waited for; matrix products, arithmetic and copies ran while one was open for 0% of the time, Pallas kernels for 0%

commit v1 on v0

v1 whole, which is shorter than its diff:
```python
import jax
import jax.numpy as jnp
from jax import lax
from jax.experimental import pallas as pl
from jax.experimental.pallas import tpu as pltpu
from jax.sharding import PartitionSpec as P

D = 4096
STEPS_DONE = 10
MESH = pl.DeviceIdType.MESH

learn_rate = 0.01
tiny_eps = 1e-30
DECAY = 1.0 - STEPS_DONE ** (-0.8)

TOK = 768
FEAT = 1024
STEPS = 8
WIDE = 256
ROWS = 64


def kernel(
    a_ref, b_ref, w_ref, rm_ref, cm_ref,
    nw_ref, up_ref, nr_ref, nc_ref,
    aa, bb, ps, own, give, take, in1, mid, in2, res, fin, grad,
    row_in, col_mine, col_in, col_mid, col_in2, sca_mine, sca_in, sca_mid, sca_in2,
    s_a, r_a, s_b1, r_b1, s_b2, r_b2, r_ps, s_fw,
    s_core, r_core, s_1, r_1, s_2, r_2, s_z, r_z,
    s_row, r_row, s_col, r_col, s_col2, r_col2, s_sca, r_sca, s_sca2, r_sca2,
):
    d = lax.axis_index("dp")
    c = lax.axis_index("mp")
    zh, x, y, core = d // 32, (d // 8) % 4, (d // 2) % 4, d % 2

    def dev(zh_, x_, y_, core_, c_):
        return (((zh_ * 4 + x_) * 4 + y_) * 2 + core_, c_)

    def plane_peer(j):
        q = lax.rem(x * 4 + y + j, 16)
        return dev(zh, q // 4, q % 4, core, c)

    def pole_peer(j):
        q = lax.rem((zh * 4 + c) * 2 + core + j, 16)
        return dev(q // 8, x, y, q % 2, (q // 2) % 4)

    def send(src, dst, s_sem, r_sem, to):
        return pltpu.make_async_remote_copy(
            src_ref=src, dst_ref=dst, send_sem=s_sem, recv_sem=r_sem, device_id=to, device_id_type=MESH
        )

    barrier = pltpu.get_barrier_semaphore()

    def greet(j, _):
        pl.semaphore_signal(barrier, inc=1, device_id=plane_peer(j), device_id_type=MESH)
        pl.semaphore_signal(barrier, inc=1, device_id=pole_peer(j), device_id_type=MESH)
        return 0

    lax.fori_loop(1, 16, greet, 0)
    pl.semaphore_wait(barrier, 30)

    edge = (c == 0) | (c == 3)
    half = lax.rem(c, 2)
    to_pair = dev(zh, x, y, core, c + 1 - 2 * half)
    to_mid = dev(zh, x, y, core, 3 - c)

    def a_copy(i):
        return send(a_ref.at[:, pl.ds(512 * i, 512)], aa.at[2 * half + i], s_a.at[i], r_a.at[i], to_pair)

    def b1_copy(i):
        return send(b_ref.at[:, pl.ds(WIDE * i, WIDE)], bb.at[i], s_b1.at[i], r_b1.at[i], to_mid)

    def b_piece(i):
        return b_ref.at[:, pl.ds(128 * i, 128)]

    def bb_piece(i):
        return bb.at[4 + i // 2, :, pl.ds(128 * (i % 2), 128)]

    def ps_piece(i):
        return ps.at[i // 2, :, pl.ds(128 * (i % 2), 128)]

    def b2_copy(i):
        return send(b_piece(i), bb_piece(i), s_b2.at[i], r_b2.at[i], to_pair)

    def ps_copy(i):
        return send(b_piece(i), ps_piece(i), s_b2.at[i], r_ps.at[i], to_pair)

    def fw_copy(i):
        return send(ps_piece(i), bb_piece(i), s_fw.at[i], r_b2.at[i], to_mid)

    @pl.when(edge)
    def _():
        for i in range(2):
            a_copy(i).start()
        for i in range(8):
            ps_copy(i).start()

    @pl.when(jnp.logical_not(edge))
    def _():
        for i in range(2):
            a_copy(i).start()
            b1_copy(2 * i).start()
            b1_copy(2 * i + 1).start()
        for i in range(8):
            b2_copy(i).start()

    for i in range(2):
        aa[2 * half + i] = a_ref[:, pl.ds(512 * i, 512)]

    @pl.when(edge)
    def _():
        for i in range(4):
            bb[i] = b_ref[:, pl.ds(WIDE * i, WIDE)]

    for i in range(2):
        send(a_ref.at[:, pl.ds(512 * i, 512)], aa.at[2 * (1 - half) + i], s_a.at[i], r_a.at[i], to_pair).wait_recv()

    def forward(i):
        @pl.when(jnp.logical_not(edge))
        def _():
            for k in range(8):
                @pl.when(i == k)
                def _():
                    ps_copy(k).wait_recv()
                    fw_copy(k).start()

    def core_copy(t):
        return send(give.at[t % 2], take.at[t], s_core.at[t], r_core.at[t], dev(zh, x, y, 1 - core, c))

    def multiply(t):
        @pl.when((t < 4) & jnp.logical_not(edge))
        def _():
            for k in range(4):
                @pl.when(t == k)
                def _():
                    b1_copy(k).wait_recv()

        for k in range(4, 8):
            @pl.when(t == k)
            def _():
                b2_copy(2 * (k - 4)).wait_recv()
                b2_copy(2 * (k - 4) + 1).wait_recv()

        @pl.when(t >= 2)
        def _():
            core_copy(t - 2).wait_send()

        def of_x(xx, _):
            r = lax.dot_general(
                aa[xx], bb[t], (((0,), (0,)), ((), ())), preferred_element_type=jnp.float32
            )
            for yy in range(4):
                lo, hi = r[128 * yy : 128 * yy + 64], r[128 * yy + 64 : 128 * yy + 128]
                keep, go = jnp.where(core == 0, lo, hi), jnp.where(core == 0, hi, lo)
                own[t, 0, xx, yy] = keep[:, :128]
                own[t, 1, yy, xx] = keep[:, 128:]
                give[t % 2, 0, xx, yy] = go[:, :128]
                give[t % 2, 1, yy, xx] = go[:, 128:]
            return 0

        lax.fori_loop(0, 4, of_x, 0)
        core_copy(t).start()

    def copies_1(t):
        out = []
        for j in range(1, 4):
            out.append(send(own.at[t, 0, lax.rem(x + j, 4)], in1.at[t, 0, j - 1], s_1.at[t, 0, j - 1],
                            r_1.at[t, 0, j - 1], dev(zh, lax.rem(x + j, 4), y, core, c)))
            out.append(send(own.at[t, 1, lax.rem(y + j, 4)], in1.at[t, 1, j - 1], s_1.at[t, 1, j - 1],
                            r_1.at[t, 1, j - 1], dev(zh, x, lax.rem(y + j, 4), core, c)))
        return out

    def add_cores(t):
        core_copy(t).wait_recv()

        def of(k, _):
            own[t, k // 4, k % 4] += take[t, k // 4, k % 4]
            return 0

        lax.fori_loop(0, 8, of, 0)
        for q in copies_1(t):
            q.start()

    def copies_2(t):
        out = []
        for j in range(1, 4):
            out.append(send(mid.at[t, 0, lax.rem(y + j, 4)], in2.at[t, 0, j - 1], s_2.at[t, 0, j - 1],
                            r_2.at[t, 0, j - 1], dev(zh, x, lax.rem(y + j, 4), core, c)))
            out.append(send(mid.at[t, 1, lax.rem(x + j, 4)], in2.at[t, 1, j - 1], s_2.at[t, 1, j - 1],
                            r_2.at[t, 1, j - 1], dev(zh, lax.rem(x + j, 4), y, core, c)))
        return out

    def add_first(t):
        for q in copies_1(t):
            q.wait_recv()
        mid[t, 0] = own[t, 0, x] + in1[t, 0, 0] + in1[t, 0, 1] + in1[t, 0, 2]
        mid[t, 1] = own[t, 1, y] + in1[t, 1, 0] + in1[t, 1, 1] + in1[t, 1, 2]
        for q in copies_2(t):
            q.start()

    def target(t):
        return jnp.where(t < 4, jnp.where(edge, c, 3 - c), lax.rem(2 * c + 1, 5))

    def stays(t):
        return (zh == c // 2) & (target(t) == c)

    def z_copy(t):
        return send(res.at[t], fin.at[zh, lax.rem(t, 4)], s_z.at[t], r_z.at[zh, lax.rem(t, 4)],
                    dev(c // 2, x, y, core, target(t)))

    def add_second(t):
        for q in copies_2(t):
            q.wait_recv()
        lo = mid[t, 0, y] + in2[t, 0, 0] + in2[t, 0, 1] + in2[t, 0, 2]
        hi = mid[t, 1, x] + in2[t, 1, 0] + in2[t, 1, 1] + in2[t, 1, 2]

        @pl.when(stays(t))
        def _():
            fin[zh, lax.rem(t, 4), :, :128] = lo
            fin[zh, lax.rem(t, 4), :, 128:] = hi

        @pl.when(jnp.logical_not(stays(t)))
        def _():
            res[t, :, :128] = lo
            res[t, :, 128:] = hi
            z_copy(t).start()

    def step(s, _):
        @pl.when(s < 8)
        def _():
            @pl.when(s >= 6)
            def _():
                forward(s)

            multiply(s)

            @pl.when(s < 6)
            def _():
                forward(s)

        @pl.when((s >= 1) & (s < 9))
        def _():
            add_cores(s - 1)

        @pl.when((s >= 2) & (s < 10))
        def _():
            add_first(s - 2)

        @pl.when(s >= 3)
        def _():
            add_second(s - 3)

        return 0

    lax.fori_loop(0, 11, step, 0)

    source = 2 * zh + c // 2
    for g in range(2):
        for k in range(4):
            @pl.when(jnp.logical_not((zh == g) & (source == c)))
            def _():
                send(res.at[k], fin.at[g, k], s_z.at[k], r_z.at[g, k], dev(g, x, y, core, source)).wait_recv()
    col_sum = []
    row_sum = jnp.zeros((ROWS, 128), jnp.float32)
    for k in range(4):
        g = fin[0, k] + fin[1, k]
        grad[:, pl.ds(WIDE * k, WIDE)] = g
        sq = g * g + tiny_eps
        row_sum = row_sum + sq[:, :128] + sq[:, 128:]
        col_mine[:, pl.ds(WIDE * k, WIDE)] = jnp.sum(sq, axis=0, keepdims=True)
    row_in[0] = row_sum

    def row_copy(j):
        return send(row_in.at[0], row_in.at[j], s_row.at[j - 1], r_row.at[j - 1], dev(zh, x, y, core, lax.rem(c + j, 4)))

    def col_copy(j):
        return send(col_mine, col_in.at[j - 1], s_col.at[j - 1], r_col.at[j - 1], plane_peer(j))

    def col_copy2(j):
        q = lax.rem(zh * 2 + core + j, 4)
        return send(col_mid, col_in2.at[j - 1], s_col2.at[j - 1], r_col2.at[j - 1], dev(q // 2, x, y, q % 2, c))

    def each(lo, hi, f):
        def one(j, _):
            f(j)
            return 0
        lax.fori_loop(lo, hi, one, 0)

    each(1, 16, lambda j: col_copy(j).start())
    each(1, 4, lambda j: row_copy(j).start())
    each(1, 16, lambda j: col_copy(j).wait_recv())
    total = col_mine[...]
    for j in range(15):
        total = total + col_in[j]
    col_mid[...] = total
    each(1, 4, lambda j: col_copy2(j).start())
    each(1, 4, lambda j: row_copy(j).wait_recv())
    rows = jnp.sum(row_in[0] + row_in[1] + row_in[2] + row_in[3], axis=1, keepdims=True)
    eye = lax.broadcasted_iota(jnp.int32, (ROWS, ROWS), 0) == lax.broadcasted_iota(jnp.int32, (ROWS, ROWS), 1)
    rm = jnp.sum(jnp.where(eye, rm_ref[...], 0.0), axis=1, keepdims=True)
    new_row = DECAY * rm + (1.0 - DECAY) * (rows / D)
    nr_ref[...] = jnp.sum(jnp.where(eye, new_row, 0.0), axis=0, keepdims=True)
    each(1, 4, lambda j: col_copy2(j).wait_recv())
    cols = col_mid[...] + col_in2[0] + col_in2[1] + col_in2[2]
    new_col = DECAY * cm_ref[...] + (1.0 - DECAY) * (cols / D)
    nc_ref[...] = new_col
    root_r = 1.0 / jnp.sqrt(new_row)
    root_c = 1.0 / jnp.sqrt(new_col)
    scaled = grad[...] * root_r * root_c
    part = jnp.sum(scaled * scaled)
    row_part = jnp.sum(new_row)
    lane = lax.broadcasted_iota(jnp.int32, (8, 128), 1)
    sca_mine[...] = jnp.where(lane == 0, part, jnp.where(lane == 1, row_part, 0.0))

    def sca_copy(j):
        return send(sca_mine, sca_in.at[j - 1], s_sca.at[j - 1], r_sca.at[j - 1], plane_peer(j))

    def sca_copy2(j):
        return send(sca_mid, sca_in2.at[j - 1], s_sca2.at[j - 1], r_sca2.at[j - 1], pole_peer(j))

    each(1, 16, lambda j: sca_copy(j).start())
    each(1, 16, lambda j: sca_copy(j).wait_recv())
    total = sca_mine[...]
    for j in range(15):
        total = total + sca_in[j]
    sca_mid[...] = total
    each(1, 16, lambda j: sca_copy2(j).start())
    each(1, 16, lambda j: sca_copy2(j).wait_recv())
    total = sca_mid[...]
    for j in range(15):
        total = total + sca_in2[j]
    sum_sq = jnp.sum(jnp.where(lane == 0, total, 0.0), axis=1, keepdims=True)[:1]
    sum_row = jnp.sum(jnp.where(lane == 1, total, 0.0), axis=1, keepdims=True)[:1] / 4.0
    scale_total = sum_row / D
    root_mean = jnp.sqrt(sum_sq * scale_total / (D * D))
    factor = jnp.sqrt(scale_total) / jnp.maximum(1.0, root_mean)
    update = grad[...] * (root_r * factor) * root_c
    up_ref[...] = update
    nw_ref[...] = w_ref[...] - learn_rate * update

    for i in range(2):
        a_copy(i).wait_send()
    for i in range(8):
        b2_copy(i).wait_send()

    @pl.when(jnp.logical_not(edge))
    def _():
        for i in range(4):
            b1_copy(i).wait_send()
        for i in range(8):
            fw_copy(i).wait_send()

    core_copy(6).wait_send()
    core_copy(7).wait_send()

    def sent(t):
        for q in copies_1(t) + copies_2(t):
            q.wait_send()

        @pl.when(jnp.logical_not(stays(t)))
        def _():
            z_copy(t).wait_send()

    each(0, 8, sent)
    each(1, 4, lambda j: row_copy(j).wait_send())
    each(1, 16, lambda j: col_copy(j).wait_send())
    each(1, 4, lambda j: col_copy2(j).wait_send())
    each(1, 16, lambda j: sca_copy(j).wait_send())
    each(1, 16, lambda j: sca_copy2(j).wait_send())


def body(activations, out_grads, weight, row_moment, col_moment):
    f32, bf16 = jnp.float32, jnp.bfloat16
    V, S = pltpu.VMEM, pltpu.SemaphoreType.DMA
    vmem = pl.BlockSpec(memory_space=pltpu.VMEM)
    buffers = [
        V((4, TOK, 512), bf16),
        V((8, TOK, WIDE), bf16),
        V((4, TOK, WIDE), bf16),
        V((STEPS, 2, 4, 4, ROWS, 128), f32),
        V((2, 2, 4, 4, ROWS, 128), f32),
        V((STEPS, 2, 4, 4, ROWS, 128), f32),
        V((STEPS, 2, 3, 4, ROWS, 128), f32),
        V((STEPS, 2, 4, ROWS, 128), f32),
        V((STEPS, 2, 3, ROWS, 128), f32),
        V((STEPS, ROWS, WIDE), f32),
        V((2, 4, ROWS, WIDE), f32),
        V((ROWS, FEAT), f32),
        V((4, ROWS, 128), f32),
        V((1, FEAT), f32), V((15, 1, FEAT), f32), V((1, FEAT), f32), V((3, 1, FEAT), f32),
        V((8, 128), f32), V((15, 8, 128), f32), V((8, 128), f32), V((15, 8, 128), f32),
    ]
    sems = [S((2,)), S((2,)), S((4,)), S((4,)), S((8,)), S((8,)), S((8,)), S((8,)),
            S((8,)), S((8,)), S((8, 2, 3)), S((8, 2, 3)), S((8, 2, 3)), S((8, 2, 3)), S((8,)), S((2, 4)),
            S((3,)), S((3,)), S((15,)), S((15,)), S((3,)), S((3,)), S((15,)), S((15,)), S((15,)), S((15,))]
    nw, up, nr, nc = pl.pallas_call(
        kernel,
        out_shape=[
            jax.ShapeDtypeStruct((ROWS, FEAT), f32),
            jax.ShapeDtypeStruct((ROWS, FEAT), f32),
            jax.ShapeDtypeStruct((1, ROWS), f32),
            jax.ShapeDtypeStruct((1, FEAT), f32),
        ],
        in_specs=[vmem] * 5,
        out_specs=[vmem] * 4,
        scratch_shapes=buffers + sems,
        compiler_params=pltpu.CompilerParams(
            collective_id=0, has_side_effects=True, vmem_limit_bytes=60 * 2**20
        ),
    )(activations, out_grads, weight, row_moment.reshape(1, ROWS), col_moment.reshape(1, FEAT))
    return nw, up, nr.reshape(ROWS), nc.reshape(FEAT)


def solution(mesh):
    return jax.shard_map(
        body,
        mesh=mesh,
        in_specs=(P("dp", "mp"), P("dp", "mp"), P("dp", "mp"), P("dp"), P("mp")),
        out_specs=(P("dp", "mp"), P("dp", "mp"), P("dp"), P("mp")),
        check_vma=False,
    )
```

time: 886 us -> 156 us (0.18)
  waiting for transfers between devices: 557 us -> 0 us
  blocking collectives: 295 us -> 0 us
  Pallas kernels: 0 us -> 149 us
  between operations: 15.4 us -> 0.64 us
  matrix products: 13 us -> 0 us
    reduce_scatter x1 -> x0, waiting for transfers between devices: 432 us -> none  [body(): lax.psum_scatter(partial_grad, 'dp', scatter_dimension=0, tiled=True)]
    psum x3 -> x0, blocking collectives: 295 us -> none  [the longest x1 214 us: body(): lax.psum((jnp.sum(squared, axis=0), jnp.sum(new_row)), 'dp')]
    pallas_call x0 -> x1, Pallas kernels: none -> 149 us  [body(): pl.pallas_call(kernel, out_shape=[jax.ShapeDtypeStruct((ROWS, FEAT), f32)...]
    all_gather x1 -> x0, waiting for transfers between devices: 124 us -> none  [body(): lax.all_gather(activations, 'mp', axis=1, tiled=True)]
    dot_general x1 -> x0, matrix products: 13 us -> none  [body(): lax.dot_general(lax.all_gather(activations, 'mp', axis=1, tiled=True), ou...]
  transfers between devices with their start and end apart: 2 -> 0, of which waited for: 2 -> 0; matrix products, arithmetic and copies ran while one was open for 0% -> 0% of each run, Pallas kernels for 0% -> 0%
where the time goes in v1:
time: 156 us
  Pallas kernels  149 us (96%)
  local copies, waits for them, and re-layouts  5.79 us (4%)
    pallas_call x1, Pallas kernels, body(): pl.pallas_call(kernel, out_shape=[jax.ShapeDtypeStruct((ROWS, FEAT), f32)...  149 us
    unnamed x4, local copies, waits for them, and re-layouts  5.79 us

profile of v1, /device:TPU:1, one launch (start us, length us, event | category | flops | bytes accessed | tf_op | source)
XLA Modules:
  0.0 155.9 jit_solution(14409216595633323089)
XLA Ops:
  0.6 149.5 %shard_map.84 = (f32[64,1024]{1,0:T(8,128)}, f32[64,1024]{1,0:T(8,128)}, f32[1,64]{1,0:T(1,128)}, f32[1,1024]{1,0:T(1,128)}) custom-call(bf16[768,1024]{1,0:T(8,128)(2,1)} %a_ref.1, bf16[768,1024]{1,0:T(8,128)(2,1)} %b_ref.1, f32[64,1024]{1,0:T(8,128)} %w_ref.1, f32[1,64]{1,0:T(1,128)} %bitcast.6, f32[1,1024]{1,0:T(1,128)} %bitcast.4), custom_call_target="tpu_custom_call" | custom-call | tf_op jit(solution)/shard_map/pallas_call | solution.py:396
  150.1 1.7 %copy.13 = f32[64,1024]{1,0:T(8,128)} copy(f32[64,1024]{1,0:T(8,128)} %get-tuple-element.16) | data formatting | bytes 524288
  151.8 1.7 %copy.14 = f32[64,1024]{1,0:T(8,128)} copy(f32[64,1024]{1,0:T(8,128)} %get-tuple-element.17) | data formatting | bytes 524288
  153.5 1.2 copy.15
  154.7 1.3 copy.16

commit v2 on v1

v2 whole, which is shorter than its diff:
```python
import jax
import jax.numpy as jnp
from jax import lax
from jax.experimental import pallas as pl
from jax.experimental.pallas import tpu as pltpu
from jax.sharding import PartitionSpec as P

D = 4096
STEPS_DONE = 10
MESH = pl.DeviceIdType.MESH

learn_rate = 0.01
tiny_eps = 1e-30
DECAY = 1.0 - STEPS_DONE ** (-0.8)

TOK = 768
FEAT = 1024
STEPS = 8
WIDE = 256
ROWS = 64


POWER = 16
TOP = 239.0


def coded(v):
    most = jnp.max(jnp.abs(v), axis=0, keepdims=True)
    scale = (most * 1.01 + 1e-30).astype(jnp.bfloat16)
    u = v * (TOP / scale.astype(jnp.float32))
    m = u * u
    m = m * m
    m = m * m
    m = m * m
    y = jnp.where(u < 0.0, -m, m).astype(jnp.bfloat16)
    return y, jnp.broadcast_to(scale, (16, v.shape[1]))


def decoded(y, scale):
    f = y.astype(jnp.float32)
    m = jnp.exp(jnp.log(jnp.abs(f)) * (1.0 / POWER))
    return jnp.where(f < 0.0, -m, m) * (scale.astype(jnp.float32)[:1] * (1.0 / TOP))


def kernel(
    a_ref, b_ref, rm_ref, cm_ref,
    grad_out, by_row_ref, by_col_ref, nr_ref, nc_ref,
    aa, bb, ps, own, give, take, enc, in1, mid, in2, res, fin, grad,
    row_in, col_mine, col_in, col_mid, col_in2, sca_mine, sca_in, sca_mid, sca_in2,
    s_loc, s_a, r_a, s_b1, r_b1, s_b2, r_b2, r_ps, s_fw,
    s_core, r_core, s_1, r_1, s_2, r_2, s_z, r_z, s_row, s_col, r_row, r_col, s_col2, r_col2, s_sca, r_sca, s_sca2, r_sca2,
):
    d = lax.axis_index("dp")
    c = lax.axis_index("mp")
    zh, x, y, core = d // 32, (d // 8) % 4, (d // 2) % 4, d % 2

    def dev(zh_, x_, y_, core_, c_):
        return (((zh_ * 4 + x_) * 4 + y_) * 2 + core_, c_)

    def plane_peer(j):
        q = lax.rem(x * 4 + y + j, 16)
        return dev(zh, q // 4, q % 4, core, c)

    def pole_peer(j):
        q = lax.rem((zh * 4 + c) * 2 + core + j, 16)
        return dev(q // 8, x, y, q % 2, (q // 2) % 4)

    def send(src, dst, s_sem, r_sem, to):
        return pltpu.make_async_remote_copy(
            src_ref=src, dst_ref=dst, send_sem=s_sem, recv_sem=r_sem, device_id=to, device_id_type=MESH
        )

    def arrived(ref, sem):
        pltpu.make_async_copy(ref, ref, sem).wait()

    barrier = pltpu.get_barrier_semaphore()

    def greet(j, _):
        pl.semaphore_signal(barrier, inc=1, device_id=plane_peer(j), device_id_type=MESH)
        pl.semaphore_signal(barrier, inc=1, device_id=pole_peer(j), device_id_type=MESH)
        return 0

    lax.fori_loop(1, 16, greet, 0)
    pl.semaphore_wait(barrier, 30)

    edge = (c == 0) | (c == 3)
    half = lax.rem(c, 2)
    to_pair = dev(zh, x, y, core, c + 1 - 2 * half)
    to_mid = dev(zh, x, y, core, 3 - c)

    def a_copy(i):
        return send(a_ref.at[:, pl.ds(512 * i, 512)], aa.at[2 * half + i], s_a, r_a, to_pair)

    def b1_copy(i):
        return send(b_ref.at[:, pl.ds(WIDE * i, WIDE)], bb.at[i], s_b1, r_b1.at[i], to_mid)

    def b_piece(i):
        return b_ref.at[:, pl.ds(128 * i, 128)]

    def bb_piece(i):
        return bb.at[4 + i // 2, :, pl.ds(128 * (i % 2), 128)]

    def ps_piece(i):
        return ps.at[i // 2, :, pl.ds(128 * (i % 2), 128)]

    def b2_copy(i):
        return send(b_piece(i), bb_piece(i), s_b2, r_b2.at[i // 2], to_pair)

    def ps_copy(i):
        return send(b_piece(i), ps_piece(i), s_b2, r_ps.at[i], to_pair)

    def fw_copy(i):
        return send(ps_piece(i), bb_piece(i), s_fw, r_b2.at[i // 2], to_mid)

    @pl.when(edge)
    def _():
        for i in range(2):
            a_copy(i).start()
        for i in range(8):
            ps_copy(i).start()

    @pl.when(jnp.logical_not(edge))
    def _():
        for i in range(2):
            a_copy(i).start()
            b1_copy(2 * i).start()
            b1_copy(2 * i + 1).start()
        for i in range(8):
            b2_copy(i).start()

    def a_local(i):
        return pltpu.make_async_copy(a_ref.at[:, pl.ds(512 * i, 512)], aa.at[2 * half + i], s_loc.at[i])

    def b_local(i):
        return pltpu.make_async_copy(b_ref.at[:, pl.ds(WIDE * i, WIDE)], bb.at[i], s_loc.at[2 + i])

    for i in range(2):
        a_local(i).start()

    @pl.when(edge)
    def _():
        for i in range(4):
            b_local(i).start()
        for i in range(4):
            b_local(i).wait()

    for i in range(2):
        a_local(i).wait()
    arrived(aa.at[pl.ds(0, 2)], r_a)

    def forward(i):
        @pl.when(jnp.logical_not(edge))
        def _():
            for k in range(8):
                @pl.when(i == k)
                def _():
                    ps_copy(k).wait_recv()
                    fw_copy(k).start()

    def core_copy(t):
        return send(give.at[t % 2], take.at[t], s_core.at[t % 2], r_core.at[t], dev(zh, x, y, 1 - core, c))

    def multiply(t):
        @pl.when((t < 4) & jnp.logical_not(edge))
        def _():
            for k in range(4):
                @pl.when(t == k)
                def _():
                    b1_copy(k).wait_recv()

        for k in range(4, 8):
            @pl.when(t == k)
            def _():
                arrived(bb.at[k], r_b2.at[k - 4])

        @pl.when(t >= 2)
        def _():
            core_copy(t - 2).wait_send()

        def of_x(xx, _):
            r = lax.dot_general(
                aa[xx], bb[t], (((0,), (0,)), ((), ())), preferred_element_type=jnp.float32
            )
            for yy in range(4):
                lo, hi = r[128 * yy : 128 * yy + 64], r[128 * yy + 64 : 128 * yy + 128]
                keep, go = jnp.where(core == 0, lo, hi), jnp.where(core == 0, hi, lo)
                own[t, 0, xx, yy] = keep[:, :128]
                own[t, 1, yy, xx] = keep[:, 128:]
                give[t % 2, 0, xx, yy] = go[:, :128]
                give[t % 2, 1, yy, xx] = go[:, 128:]
            return 0

        lax.fori_loop(0, 4, of_x, 0)
        core_copy(t).start()

    def copies_1(t):
        out = []
        for j in range(1, 4):
            out.append(send(enc.at[t, 0, lax.rem(x + j, 4)], in1.at[t, 0, j - 1], s_1.at[t], r_1.at[t],
                            dev(zh, lax.rem(x + j, 4), y, core, c)))
            out.append(send(enc.at[t, 1, lax.rem(y + j, 4)], in1.at[t, 1, j - 1], s_1.at[t], r_1.at[t],
                            dev(zh, x, lax.rem(y + j, 4), core, c)))
        return out

    def add_cores(t):
        core_copy(t).wait_recv()

        def of(k, _):
            v = own[t, k // 4, k % 4] + take[t, k // 4, k % 4]
            own[t, k // 4, k % 4] = v
            code, scale = coded(v.reshape(4 * ROWS, 128))
            enc[t, k // 4, k % 4, : 4 * ROWS] = code
            enc[t, k // 4, k % 4, 4 * ROWS :] = scale
            return 0

        lax.fori_loop(0, 8, of, 0)
        for q in copies_1(t):
            q.start()

    def copies_2(t):
        out = []
        for j in range(1, 4):
            out.append(send(mid.at[t, 0, lax.rem(y + j, 4)], in2.at[t, 0, j - 1], s_2.at[t], r_2.at[t], dev(zh, x, lax.rem(y + j, 4), core, c)))
            out.append(send(mid.at[t, 1, lax.rem(x + j, 4)], in2.at[t, 1, j - 1], s_2.at[t], r_2.at[t], dev(zh, lax.rem(x + j, 4), y, core, c)))
        return out

    def add_first(t):
        arrived(in1.at[t], r_1.at[t])

        def of(h, _):
            total = own[t, h, jnp.where(h == 0, x, y)].reshape(4 * ROWS, 128)
            for k in range(3):
                total = total + decoded(in1[t, h, k, : 4 * ROWS], in1[t, h, k, 4 * ROWS :])
            mid[t, h] = total.reshape(4, ROWS, 128)
            return 0

        lax.fori_loop(0, 2, of, 0)
        for q in copies_2(t):
            q.start()

    def target(t):
        return jnp.where(t < 4, jnp.where(edge, c, 3 - c), lax.rem(2 * c + 1, 5))

    def stays(t):
        return (zh == c // 2) & (target(t) == c)

    def z_copy(t):
        return send(res.at[t], fin.at[zh, lax.rem(t, 4)], s_z, r_z.at[zh],
                    dev(c // 2, x, y, core, target(t)))

    def add_second(t):
        arrived(in2.at[t], r_2.at[t])
        lo = mid[t, 0, y] + in2[t, 0, 0] + in2[t, 0, 1] + in2[t, 0, 2]
        hi = mid[t, 1, x] + in2[t, 1, 0] + in2[t, 1, 1] + in2[t, 1, 2]
        (lo, lo_scale), (hi, hi_scale) = coded(lo), coded(hi)

        def put(ref):
            ref[:ROWS, :128] = lo
            ref[:ROWS, 128:] = hi
            ref[ROWS:, :128] = lo_scale
            ref[ROWS:, 128:] = hi_scale

        @pl.when(stays(t))
        def _():
            put(fin.at[zh, lax.rem(t, 4)])

        @pl.when(jnp.logical_not(stays(t)))
        def _():
            put(res.at[t])
            z_copy(t).start()

    def step(s, _):
        @pl.when(s < 8)
        def _():
            @pl.when(s >= 6)
            def _():
                forward(s)

            multiply(s)

            @pl.when(s < 6)
            def _():
                forward(s)

        @pl.when((s >= 1) & (s < 9))
        def _():
            add_cores(s - 1)

        @pl.when((s >= 2) & (s < 10))
        def _():
            add_first(s - 2)

        @pl.when(s >= 3)
        def _():
            add_second(s - 3)

        return 0

    lax.fori_loop(0, 11, step, 0)

    source = 2 * zh + c // 2
    for g in range(2):
        @pl.when(jnp.logical_not((zh == g) & (source == c)))
        def _():
            arrived(fin.at[g], r_z.at[g])
    row_sum = jnp.zeros((ROWS, 128), jnp.float32)
    for k in range(4):
        g = decoded(fin[0, k, :ROWS], fin[0, k, ROWS:]) + decoded(fin[1, k, :ROWS], fin[1, k, ROWS:])
        grad[:, pl.ds(WIDE * k, WIDE)] = g
        sq = g * g + tiny_eps
        row_sum = row_sum + sq[:, :128] + sq[:, 128:]
        col_mine[:, pl.ds(WIDE * k, WIDE)] = jnp.sum(sq, axis=0, keepdims=True)
    row_in[0] = row_sum
    grad_copy = pltpu.make_async_copy(grad, grad_out, s_loc.at[0])
    grad_copy.start()

    def row_copy(j):
        return send(row_in.at[0], row_in.at[j], s_row, r_row, dev(zh, x, y, core, lax.rem(c + j, 4)))

    def col_copy(j):
        return send(col_mine, col_in.at[j - 1], s_col, r_col, plane_peer(j))

    def col_copy2(j):
        q = lax.rem(zh * 2 + core + j, 4)
        return send(col_mid, col_in2.at[j - 1], s_col2, r_col2, dev(q // 2, x, y, q % 2, c))

    def each(lo, hi, f):
        def one(j, _):
            f(j)
            return 0
        lax.fori_loop(lo, hi, one, 0)

    each(1, 16, lambda j: col_copy(j).start())
    each(1, 4, lambda j: row_copy(j).start())
    arrived(col_in, r_col)
    total = col_mine[...]
    for j in range(15):
        total = total + col_in[j]
    col_mid[...] = total
    each(1, 4, lambda j: col_copy2(j).start())
    arrived(row_in.at[pl.ds(1, 3)], r_row)
    rows = jnp.sum(row_in[0] + row_in[1] + row_in[2] + row_in[3], axis=1, keepdims=True)
    eye = lax.broadcasted_iota(jnp.int32, (ROWS, ROWS), 0) == lax.broadcasted_iota(jnp.int32, (ROWS, ROWS), 1)
    rm = jnp.sum(jnp.where(eye, rm_ref[...], 0.0), axis=1, keepdims=True)
    new_row = DECAY * rm + (1.0 - DECAY) * (rows / D)
    nr_ref[...] = jnp.sum(jnp.where(eye, new_row, 0.0), axis=0, keepdims=True)
    arrived(col_in2, r_col2)
    cols = col_mid[...] + col_in2[0] + col_in2[1] + col_in2[2]
    new_col = DECAY * cm_ref[...] + (1.0 - DECAY) * (cols / D)
    nc_ref[...] = new_col
    root_r = 1.0 / jnp.sqrt(new_row)
    root_c = 1.0 / jnp.sqrt(new_col)
    scaled = grad[...] * root_r * root_c
    part = jnp.sum(scaled * scaled)
    row_part = jnp.sum(new_row)
    lane = lax.broadcasted_iota(jnp.int32, (8, 128), 1)
    sca_mine[...] = jnp.where(lane == 0, part, jnp.where(lane == 1, row_part, 0.0))

    def sca_copy(j):
        return send(sca_mine, sca_in.at[j - 1], s_sca, r_sca, plane_peer(j))

    def sca_copy2(j):
        return send(sca_mid, sca_in2.at[j - 1], s_sca2, r_sca2, pole_peer(j))

    each(1, 16, lambda j: sca_copy(j).start())
    arrived(sca_in, r_sca)
    total = sca_mine[...]
    for j in range(15):
        total = total + sca_in[j]
    sca_mid[...] = total
    each(1, 16, lambda j: sca_copy2(j).start())
    arrived(sca_in2, r_sca2)
    total = sca_mid[...]
    for j in range(15):
        total = total + sca_in2[j]
    sum_sq = jnp.sum(jnp.where(lane == 0, total, 0.0), axis=1, keepdims=True)[:1]
    sum_row = jnp.sum(jnp.where(lane == 1, total, 0.0), axis=1, keepdims=True)[:1] / 4.0
    scale_total = sum_row / D
    root_mean = jnp.sqrt(sum_sq * scale_total / (D * D))
    factor = jnp.sqrt(scale_total) / jnp.maximum(1.0, root_mean)
    by_row_ref[...] = jnp.broadcast_to(root_r * factor, (ROWS, 128))
    by_col_ref[...] = root_c

    grad_copy.wait()
    arrived(aa.at[pl.ds(0, 2)], s_a)
    arrived(bb.at[pl.ds(4, 4)], s_b2)

    @pl.when(jnp.logical_not(edge))
    def _():
        arrived(bb.at[pl.ds(0, 4)], s_b1)
        arrived(bb.at[pl.ds(4, 4)], s_fw)

    core_copy(6).wait_send()
    core_copy(7).wait_send()

    def sent(t):
        arrived(in1.at[t], s_1.at[t])
        arrived(in2.at[t], s_2.at[t])

        @pl.when(jnp.logical_not(stays(t)))
        def _():
            z_copy(t).wait_send()

    each(0, 8, sent)
    arrived(row_in.at[pl.ds(1, 3)], s_row)
    arrived(col_in, s_col)
    arrived(col_in2, s_col2)
    arrived(sca_in, s_sca)
    arrived(sca_in2, s_sca2)


def finish(grad_ref, by_row_ref, by_col_ref, w_ref, nr_in, nc_in, nw_ref, up_ref, nr_ref, nc_ref):
    scale = by_row_ref[...]
    for k in range(8):
        at = pl.ds(128 * k, 128)
        update = grad_ref[:, at] * scale * by_col_ref[:, at]
        up_ref[:, at] = update
        nw_ref[:, at] = w_ref[:, at] - learn_rate * update
    nr_ref[...] = nr_in[...]
    nc_ref[...] = nc_in[...]


def body(activations, out_grads, weight, row_moment, col_moment):
    f32, bf16 = jnp.float32, jnp.bfloat16
    V, S = pltpu.VMEM, pltpu.SemaphoreType.DMA
    vmem, hbm = pl.BlockSpec(memory_space=pltpu.VMEM), pl.BlockSpec(memory_space=pl.ANY)
    buffers = [
        V((4, TOK, 512), bf16),
        V((8, TOK, WIDE), bf16),
        V((4, TOK, WIDE), bf16),
        V((STEPS, 2, 4, 4, ROWS, 128), f32),
        V((2, 2, 4, 4, ROWS, 128), f32),
        V((STEPS, 2, 4, 4, ROWS, 128), f32),
        V((STEPS, 2, 4, 4 * ROWS + 16, 128), bf16),
        V((STEPS, 2, 3, 4 * ROWS + 16, 128), bf16),
        V((STEPS, 2, 4, ROWS, 128), f32),
        V((STEPS, 2, 3, ROWS, 128), f32),
        V((STEPS, ROWS + 16, WIDE), bf16),
        V((2, 4, ROWS + 16, WIDE), bf16),
        V((ROWS, FEAT), f32),
        V((4, ROWS, 128), f32),
        V((1, FEAT), f32), V((15, 1, FEAT), f32), V((1, FEAT), f32), V((3, 1, FEAT), f32),
        V((8, 128), f32), V((15, 8, 128), f32), V((8, 128), f32), V((15, 8, 128), f32),
    ]
    sems = [S((6,)), S(()), S(()), S(()), S((4,)), S(()), S((4,)), S((8,)), S(()),
            S((2,)), S((8,)), S((8,)), S((8,)), S((8,)), S((8,)), S(()), S((2,))] + [S(())] * 10
    shape = lambda *dims: jax.ShapeDtypeStruct(dims, f32)
    grad, by_row, by_col, nr, nc = pl.pallas_call(
        kernel,
        out_shape=[shape(ROWS, FEAT), shape(ROWS, 128), shape(1, FEAT), shape(1, ROWS), shape(1, FEAT)],
        in_specs=[hbm, hbm, vmem, vmem],
        out_specs=[hbm, vmem, vmem, vmem, vmem],
        scratch_shapes=buffers + sems,
        compiler_params=pltpu.CompilerParams(
            collective_id=0, has_side_effects=True, vmem_limit_bytes=60 * 2**20
        ),
    )(activations, out_grads, row_moment.reshape(1, ROWS), col_moment.reshape(1, FEAT))
    nw, up, nr, nc = pl.pallas_call(
        finish,
        out_shape=[shape(ROWS, FEAT), shape(ROWS, FEAT), shape(1, ROWS), shape(1, FEAT)],
        in_specs=[vmem] * 6,
        out_specs=[vmem] * 4,
    )(grad, by_row, by_col, weight, nr, nc)
    return nw, up, nr.reshape(ROWS), nc.reshape(FEAT)


def solution(mesh):
    return jax.shard_map(
        body,
        mesh=mesh,
        in_specs=(P("dp", "mp"), P("dp", "mp"), P("dp", "mp"), P("dp"), P("mp")),
        out_specs=(P("dp", "mp"), P("dp", "mp"), P("dp"), P("mp")),
        check_vma=False,
    )
```

time: 156 us -> 136 us (0.87)
  Pallas kernels: 149 us -> 135 us
  local copies, waits for them, and re-layouts: 5.79 us -> 0 us
    pallas_call x1 -> x2, Pallas kernels: 149 us -> 135 us  [the longest x1 133 us: body(): pl.pallas_call(kernel, out_shape=[shape(ROWS, FEAT), shape(ROWS, 128), sh...]
    unnamed x4 -> x0, local copies, waits for them, and re-layouts: 5.79 us -> none
where the time goes in v2:
time: 136 us
  Pallas kernels  135 us (99%)
    pallas_call x1, Pallas kernels, body(): pl.pallas_call(kernel, out_shape=[shape(ROWS, FEAT), shape(ROWS, 128), sh...  133 us

profile of v2, /device:TPU:1, one launch (start us, length us, event | category | flops | bytes accessed | tf_op | source)
XLA Modules:
  0.0 135.5 jit_solution(2365970591479818680)
XLA Ops:
  0.6 133.0 %shard_map.84 = (f32[64,1024]{1,0:T(8,128)}, f32[64,128]{1,0:T(8,128)}, f32[1,1024]{1,0:T(1,128)}, f32[1,64]{1,0:T(1,128)}, f32[1,1024]{1,0:T(1,128)}) custom-call(bf16[768,1024]{1,0:T(8,128)(2,1)} %a_ref.1, bf16[768,1024]{1,0:T(8,128)(2,1)} %b_ref.1, f32[1,64]{1,0:T(1,128)} %bitcast.5, f32[1,1024]{1,0:T(1,128)} %bitcast.4), custom_call_target="tpu_custom_call" | custom-call | tf_op jit(solution)/shard_map/pallas_call | solution.py:448
  133.6 1.9 %shard_map.85 = (f32[64,1024]{1,0:T(8,128)}, f32[64,1024]{1,0:T(8,128)}, f32[1,64]{1,0:T(1,128)}, f32[1,1024]{1,0:T(1,128)}) custom-call(f32[64,1024]{1,0:T(8,128)} %get-tuple-element.13.grad_ref, f32[64,128]{1,0:T(8,128)} %get-tuple-element.14.by_row_ref, f32[1,1024]{1,0:T(1,128)} %get-tuple-element.15.by_col_ref, f32[64,1024]{1,0:T(8,128)} %w_ref.1, ...), custom_call_target="tpu_custom_call" | custom-call | tf_op jit(solution)/shard_map/pallas_call | solution.py:458

commit v3 on v2

--- a/solution.py
+++ b/solution.py
@@ -48,7 +48,7 @@
     aa, bb, ps, own, give, take, enc, in1, mid, in2, res, fin, grad,
     row_in, col_mine, col_in, col_mid, col_in2, sca_mine, sca_in, sca_mid, sca_in2,
     s_loc, s_a, r_a, s_b1, r_b1, s_b2, r_b2, r_ps, s_fw,
-    s_core, r_core, s_1, r_1, s_2, r_2, s_z, r_z, s_row, s_col, r_row, r_col, s_col2, r_col2, s_sca, r_sca, s_sca2, r_sca2,
+    s_core, r_core, s_1, r_1, s_2, r_2, s_z, r_z, s_row, s_col, r_row, r_col, s_col2, r_col2, s_sca, r_sca, s_sca2, r_sca2, heard,
 ):
     d = lax.axis_index("dp")
     c = lax.axis_index("mp")
@@ -73,15 +73,22 @@
     def arrived(ref, sem):
         pltpu.make_async_copy(ref, ref, sem).wait()
 
+    up, down = lax.rem(zh * 4 + c + 1, 8), lax.rem(zh * 4 + c + 7, 8)
+    neighbours = [
+        dev(zh, x, y, 1 - core, c),
+        dev(zh, lax.rem(x + 1, 4), y, core, c), dev(zh, lax.rem(x + 3, 4), y, core, c),
+        dev(zh, x, lax.rem(y + 1, 4), core, c), dev(zh, x, lax.rem(y + 3, 4), core, c),
+        dev(up // 4, x, y, core, up % 4), dev(down // 4, x, y, core, down % 4),
+    ]
     barrier = pltpu.get_barrier_semaphore()
-
-    def greet(j, _):
-        pl.semaphore_signal(barrier, inc=1, device_id=plane_peer(j), device_id_type=MESH)
-        pl.semaphore_signal(barrier, inc=1, device_id=pole_peer(j), device_id_type=MESH)
-        return 0
-
-    lax.fori_loop(1, 16, greet, 0)
-    pl.semaphore_wait(barrier, 30)
+    for to in neighbours:
+        pl.semaphore_signal(barrier, inc=1, device_id=to, device_id_type=MESH)
+    pl.semaphore_wait(barrier, 7)
+
+    def hail(k):
+        for to in neighbours:
+            pl.semaphore_signal(heard.at[k], inc=1, device_id=to, device_id_type=MESH)
+        pl.semaphore_wait(heard.at[k], 7)
 
     edge = (c == 0) | (c == 3)
     half = lax.rem(c, 2)
@@ -141,6 +148,12 @@
     def _():
         for i in range(4):
             b_local(i).start()
+
+    for k in range(4):
+        hail(k)
+
+    @pl.when(edge)
+    def _():
         for i in range(4):
             b_local(i).wait()
 
@@ -330,44 +343,48 @@
             return 0
         lax.fori_loop(lo, hi, one, 0)
 
+    each(1, 4, lambda j: row_copy(j).start())
     each(1, 16, lambda j: col_copy(j).start())
-    each(1, 4, lambda j: row_copy(j).start())
+    eye = lax.broadcasted_iota(jnp.int32, (ROWS, ROWS), 0) == lax.broadcasted_iota(jnp.int32, (ROWS, ROWS), 1)
+    rm = jnp.sum(jnp.where(eye, rm_ref[...], 0.0), axis=1, keepdims=True)
+    arrived(row_in.at[pl.ds(1, 3)], r_row)
+    rows = jnp.sum(row_in[0] + row_in[1] + row_in[2] + row_in[3], axis=1, keepdims=True)
+    new_row = DECAY * rm + (1.0 - DECAY) * (rows / D)
+    inverse = 1.0 / new_row
+    for k in range(4):
+        g = grad[:, pl.ds(WIDE * k, WIDE)]
+        sca_mine[:, pl.ds(WIDE * k, WIDE)] = jnp.sum(g * g * inverse, axis=0, keepdims=True)
+    sca_mine[:, FEAT:] = jnp.broadcast_to(jnp.sum(new_row, axis=0, keepdims=True), (1, 128))
+
+    def sca_copy(j):
+        return send(sca_mine, sca_in.at[j - 1], s_sca, r_sca, plane_peer(j))
+
+    def sca_copy2(j):
+        return send(sca_mid, sca_in2.at[j - 1], s_sca2, r_sca2, pole_peer(j))
+
     arrived(col_in, r_col)
     total = col_mine[...]
     for j in range(15):
         total = total + col_in[j]
     col_mid[...] = total
     each(1, 4, lambda j: col_copy2(j).start())
-    arrived(row_in.at[pl.ds(1, 3)], r_row)
-    rows = jnp.sum(row_in[0] + row_in[1] + row_in[2] + row_in[3], axis=1, keepdims=True)
-    eye = lax.broadcasted_iota(jnp.int32, (ROWS, ROWS), 0) == lax.broadcasted_iota(jnp.int32, (ROWS, ROWS), 1)
-    rm = jnp.sum(jnp.where(eye, rm_ref[...], 0.0), axis=1, keepdims=True)
-    new_row = DECAY * rm + (1.0 - DECAY) * (rows / D)
+    each(1, 16, lambda j: sca_copy(j).start())
     nr_ref[...] = jnp.sum(jnp.where(eye, new_row, 0.0), axis=0, keepdims=True)
+    root_r = 1.0 / jnp.sqrt(new_row)
     arrived(col_in2, r_col2)
     cols = col_mid[...] + col_in2[0] + col_in2[1] + col_in2[2]
     new_col = DECAY * cm_ref[...] + (1.0 - DECAY) * (cols / D)
     nc_ref[...] = new_col
-    root_r = 1.0 / jnp.sqrt(new_row)
     root_c = 1.0 / jnp.sqrt(new_col)
-    scaled = grad[...] * root_r * root_c
-    part = jnp.sum(scaled * scaled)
-    row_part = jnp.sum(new_row)
-    lane = lax.broadcasted_iota(jnp.int32, (8, 128), 1)
-    sca_mine[...] = jnp.where(lane == 0, part, jnp.where(lane == 1, row_part, 0.0))
-
-    def sca_copy(j):
-        return send(sca_mine, sca_in.at[j - 1], s_sca, r_sca, plane_peer(j))
-
-    def sca_copy2(j):
-        return send(sca_mid, sca_in2.at[j - 1], s_sca2, r_sca2, pole_peer(j))
-
-    each(1, 16, lambda j: sca_copy(j).start())
+    by_col_ref[...] = root_c
+    inverse = 1.0 / new_col
     arrived(sca_in, r_sca)
     total = sca_mine[...]
     for j in range(15):
         total = total + sca_in[j]
-    sca_mid[...] = total
+    part = jnp.sum(total[:, :FEAT] * inverse, axis=1, keepdims=True)
+    lane = lax.broadcasted_iota(jnp.int32, (8, 128), 1)
+    sca_mid[...] = jnp.where(lane == 0, part, jnp.where(lane == 1, total[:, FEAT:], 0.0))
     each(1, 16, lambda j: sca_copy2(j).start())
     arrived(sca_in2, r_sca2)
     total = sca_mid[...]
@@ -379,7 +396,6 @@
     root_mean = jnp.sqrt(sum_sq * scale_total / (D * D))
     factor = jnp.sqrt(scale_total) / jnp.maximum(1.0, root_mean)
     by_row_ref[...] = jnp.broadcast_to(root_r * factor, (ROWS, 128))
-    by_col_ref[...] = root_c
 
     grad_copy.wait()
     arrived(aa.at[pl.ds(0, 2)], s_a)
@@ -440,10 +456,10 @@
         V((ROWS, FEAT), f32),
         V((4, ROWS, 128), f32),
         V((1, FEAT), f32), V((15, 1, FEAT), f32), V((1, FEAT), f32), V((3, 1, FEAT), f32),
-        V((8, 128), f32), V((15, 8, 128), f32), V((8, 128), f32), V((15, 8, 128), f32),
+        V((1, FEAT + 128), f32), V((15, 1, FEAT + 128), f32), V((8, 128), f32), V((15, 8, 128), f32),
     ]
     sems = [S((6,)), S(()), S(()), S(()), S((4,)), S(()), S((4,)), S((8,)), S(()),
-            S((2,)), S((8,)), S((8,)), S((8,)), S((8,)), S((8,)), S(()), S((2,))] + [S(())] * 10
+            S((2,)), S((8,)), S((8,)), S((8,)), S((8,)), S((8,)), S(()), S((2,))] + [S(())] * 10 + [pltpu.SemaphoreType.REGULAR((4,))]
     shape = lambda *dims: jax.ShapeDtypeStruct(dims, f32)
     grad, by_row, by_col, nr, nc = pl.pallas_call(
         kernel,

time: 136 us -> 130 us (0.956)
  Pallas kernels: 135 us -> 129 us
    pallas_call x1, Pallas kernels: 133 us -> 127 us  [body(): pl.pallas_call(kernel, out_shape=[shape(ROWS, FEAT), shape(ROWS, 128), sh...]
where the time goes in v3:
time: 130 us
  Pallas kernels  129 us (99%)
    pallas_call x1, Pallas kernels, body(): pl.pallas_call(kernel, out_shape=[shape(ROWS, FEAT), shape(ROWS, 128), sh...  127 us

profile of v3, /device:TPU:1, one launch (start us, length us, event | category | flops | bytes accessed | tf_op | source)
XLA Modules:
  0.0 130.0 jit_solution(11871251035231284080)
XLA Ops:
  0.6 127.5 %shard_map.84 = (f32[64,1024]{1,0:T(8,128)}, f32[64,128]{1,0:T(8,128)}, f32[1,1024]{1,0:T(1,128)}, f32[1,64]{1,0:T(1,128)}, f32[1,1024]{1,0:T(1,128)}) custom-call(bf16[768,1024]{1,0:T(8,128)(2,1)} %a_ref.1, bf16[768,1024]{1,0:T(8,128)(2,1)} %b_ref.1, f32[1,64]{1,0:T(1,128)} %bitcast.5, f32[1,1024]{1,0:T(1,128)} %bitcast.4), custom_call_target="tpu_custom_call" | custom-call | tf_op jit(solution)/shard_map/pallas_call | solution.py:464
  128.1 1.9 %shard_map.85 = (f32[64,1024]{1,0:T(8,128)}, f32[64,1024]{1,0:T(8,128)}, f32[1,64]{1,0:T(1,128)}, f32[1,1024]{1,0:T(1,128)}) custom-call(f32[64,1024]{1,0:T(8,128)} %get-tuple-element.13.grad_ref, f32[64,128]{1,0:T(8,128)} %get-tuple-element.14.by_row_ref, f32[1,1024]{1,0:T(1,128)} %get-tuple-element.15.by_col_ref, f32[64,1024]{1,0:T(8,128)} %w_ref.1, ...), custom_call_target="tpu_custom_call" | custom-call | tf_op jit(solution)/shard_map/pallas_call | solution.py:474

commit v4 on v3

--- a/solution.py
+++ b/solution.py
@@ -101,29 +101,32 @@
     def b1_copy(i):
         return send(b_ref.at[:, pl.ds(WIDE * i, WIDE)], bb.at[i], s_b1, r_b1.at[i], to_mid)
 
+    def piece(i):
+        return pl.ds(192 * (i % 4), 192)
+
     def b_piece(i):
-        return b_ref.at[:, pl.ds(128 * i, 128)]
+        return b_ref.at[piece(i), pl.ds(WIDE * (i // 4), WIDE)]
 
     def bb_piece(i):
-        return bb.at[4 + i // 2, :, pl.ds(128 * (i % 2), 128)]
+        return bb.at[4 + i // 4, piece(i)]
 
     def ps_piece(i):
-        return ps.at[i // 2, :, pl.ds(128 * (i % 2), 128)]
+        return ps.at[i // 4, piece(i)]
 
     def b2_copy(i):
-        return send(b_piece(i), bb_piece(i), s_b2, r_b2.at[i // 2], to_pair)
+        return send(b_piece(i), bb_piece(i), s_b2, r_b2.at[i // 4], to_pair)
 
     def ps_copy(i):
         return send(b_piece(i), ps_piece(i), s_b2, r_ps.at[i], to_pair)
 
     def fw_copy(i):
-        return send(ps_piece(i), bb_piece(i), s_fw, r_b2.at[i // 2], to_mid)
+        return send(ps_piece(i), bb_piece(i), s_fw, r_b2.at[i // 4], to_mid)
 
     @pl.when(edge)
     def _():
         for i in range(2):
             a_copy(i).start()
-        for i in range(8):
+        for i in range(16):
             ps_copy(i).start()
 
     @pl.when(jnp.logical_not(edge))
@@ -132,7 +135,7 @@
             a_copy(i).start()
             b1_copy(2 * i).start()
             b1_copy(2 * i + 1).start()
-        for i in range(8):
+        for i in range(16):
             b2_copy(i).start()
 
     def a_local(i):
@@ -161,11 +164,11 @@
         a_local(i).wait()
     arrived(aa.at[pl.ds(0, 2)], r_a)
 
-    def forward(i):
+    def forward(s, pieces):
         @pl.when(jnp.logical_not(edge))
         def _():
-            for k in range(8):
-                @pl.when(i == k)
+            for at, k in pieces:
+                @pl.when(s == at)
                 def _():
                     ps_copy(k).wait_recv()
                     fw_copy(k).start()
@@ -219,11 +222,20 @@
         core_copy(t).wait_recv()
 
         def of(k, _):
-            v = own[t, k // 4, k % 4] + take[t, k // 4, k % 4]
-            own[t, k // 4, k % 4] = v
-            code, scale = coded(v.reshape(4 * ROWS, 128))
-            enc[t, k // 4, k % 4, : 4 * ROWS] = code
-            enc[t, k // 4, k % 4, 4 * ROWS :] = scale
+            h, q = k // 4, k % 4
+            v = own[t, h, q] + take[t, h, q]
+            mine = q == jnp.where(h == 0, x, y)
+
+            @pl.when(mine)
+            def _():
+                own[t, h, q] = v
+
+            @pl.when(jnp.logical_not(mine))
+            def _():
+                code, scale = coded(v.reshape(4 * ROWS, 128))
+                enc[t, h, q, : 4 * ROWS] = code
+                enc[t, h, q, 4 * ROWS :] = scale
+
             return 0
 
         lax.fori_loop(0, 8, of, 0)
@@ -282,34 +294,22 @@
             put(res.at[t])
             z_copy(t).start()
 
+    def when(cond, f, t):
+        @pl.when(cond)
+        def _():
+            f(t)
+
     def step(s, _):
-        @pl.when(s < 8)
-        def _():
-            @pl.when(s >= 6)
-            def _():
-                forward(s)
-
-            multiply(s)
-
-            @pl.when(s < 6)
-            def _():
-                forward(s)
-
-        @pl.when((s >= 1) & (s < 9))
-        def _():
-            add_cores(s - 1)
-
-        @pl.when((s >= 2) & (s < 10))
-        def _():
-            add_first(s - 2)
-
-        @pl.when(s >= 3)
-        def _():
-            add_second(s - 3)
-
+        forward(s, [(6, 12), (6, 13), (7, 14), (7, 15)])
+        when(s < 8, multiply, s)
+        forward(s, [(k, 2 * k) for k in range(6)])
+        when((s >= 1) & (s < 9), add_cores, s - 1)
+        forward(s, [(k, 2 * k + 1) for k in range(6)])
+        when((s >= 3) & (s < 11), add_first, s - 3)
+        when(s >= 5, add_second, s - 5)
         return 0
 
-    lax.fori_loop(0, 11, step, 0)
+    lax.fori_loop(0, 13, step, 0)
 
     source = 2 * zh + c // 2
     for g in range(2):
@@ -458,7 +458,7 @@
         V((1, FEAT), f32), V((15, 1, FEAT), f32), V((1, FEAT), f32), V((3, 1, FEAT), f32),
         V((1, FEAT + 128), f32), V((15, 1, FEAT + 128), f32), V((8, 128), f32), V((15, 8, 128), f32),
     ]
-    sems = [S((6,)), S(()), S(()), S(()), S((4,)), S(()), S((4,)), S((8,)), S(()),
+    sems = [S((6,)), S(()), S(()), S(()), S((4,)), S(()), S((4,)), S((16,)), S(()),
             S((2,)), S((8,)), S((8,)), S((8,)), S((8,)), S((8,)), S(()), S((2,))] + [S(())] * 10 + [pltpu.SemaphoreType.REGULAR((4,))]
     shape = lambda *dims: jax.ShapeDtypeStruct(dims, f32)
     grad, by_row, by_col, nr, nc = pl.pallas_call(

time: 130 us -> 126 us (0.969)
  Pallas kernels: 129 us -> 125 us
    pallas_call x1, Pallas kernels: 127 us -> 123 us  [body(): pl.pallas_call(kernel, out_shape=[shape(ROWS, FEAT), shape(ROWS, 128), sh...]
where the time goes in v4:
time: 126 us
  Pallas kernels  125 us (99%)
    pallas_call x1, Pallas kernels, body(): pl.pallas_call(kernel, out_shape=[shape(ROWS, FEAT), shape(ROWS, 128), sh...  123 us

profile of v4, /device:TPU:1, one launch (start us, length us, event | category | flops | bytes accessed | tf_op | source)
XLA Modules:
  0.0 126.0 jit_solution(12001088657947783026)
XLA Ops:
  0.6 123.4 %shard_map.84 = (f32[64,1024]{1,0:T(8,128)}, f32[64,128]{1,0:T(8,128)}, f32[1,1024]{1,0:T(1,128)}, f32[1,64]{1,0:T(1,128)}, f32[1,1024]{1,0:T(1,128)}) custom-call(bf16[768,1024]{1,0:T(8,128)(2,1)} %a_ref.1, bf16[768,1024]{1,0:T(8,128)(2,1)} %b_ref.1, f32[1,64]{1,0:T(1,128)} %bitcast.5, f32[1,1024]{1,0:T(1,128)} %bitcast.4), custom_call_target="tpu_custom_call" | custom-call | tf_op jit(solution)/shard_map/pallas_call | solution.py:464
  124.1 1.9 %shard_map.85 = (f32[64,1024]{1,0:T(8,128)}, f32[64,1024]{1,0:T(8,128)}, f32[1,64]{1,0:T(1,128)}, f32[1,1024]{1,0:T(1,128)}) custom-call(f32[64,1024]{1,0:T(8,128)} %get-tuple-element.13.grad_ref, f32[64,128]{1,0:T(8,128)} %get-tuple-element.14.by_row_ref, f32[1,1024]{1,0:T(1,128)} %get-tuple-element.15.by_col_ref, f32[64,1024]{1,0:T(8,128)} %w_ref.1, ...), custom_call_target="tpu_custom_call" | custom-call | tf_op jit(solution)/shard_map/pallas_call | solution.py:474

commit v5 on v4

--- a/solution.py
+++ b/solution.py
@@ -45,9 +45,9 @@
 def kernel(
     a_ref, b_ref, rm_ref, cm_ref,
     grad_out, by_row_ref, by_col_ref, nr_ref, nc_ref,
-    aa, bb, ps, own, give, take, enc, in1, mid, in2, res, fin, grad,
+    aa, bb, own, give, take, enc, in1, mid, in2, res, fin, grad,
     row_in, col_mine, col_in, col_mid, col_in2, sca_mine, sca_in, sca_mid, sca_in2,
-    s_loc, s_a, r_a, s_b1, r_b1, s_b2, r_b2, r_ps, s_fw,
+    s_loc, s_a, r_a, s_b1, r_b1, s_b2, r_b2,
     s_core, r_core, s_1, r_1, s_2, r_2, s_z, r_z, s_row, s_col, r_row, r_col, s_col2, r_col2, s_sca, r_sca, s_sca2, r_sca2, heard,
 ):
     d = lax.axis_index("dp")
@@ -110,24 +110,16 @@
     def bb_piece(i):
         return bb.at[4 + i // 4, piece(i)]
 
-    def ps_piece(i):
-        return ps.at[i // 4, piece(i)]
-
     def b2_copy(i):
         return send(b_piece(i), bb_piece(i), s_b2, r_b2.at[i // 4], to_pair)
 
-    def ps_copy(i):
-        return send(b_piece(i), ps_piece(i), s_b2, r_ps.at[i], to_pair)
-
-    def fw_copy(i):
-        return send(ps_piece(i), bb_piece(i), s_fw, r_b2.at[i // 4], to_mid)
+    def far_copy(i):
+        return send(b_piece(i), bb_piece(i), s_b2, r_b2.at[i // 4], dev(zh, x, y, core, jnp.where(c == 0, 2, 1)))
 
     @pl.when(edge)
     def _():
         for i in range(2):
             a_copy(i).start()
-        for i in range(16):
-            ps_copy(i).start()
 
     @pl.when(jnp.logical_not(edge))
     def _():
@@ -152,7 +144,14 @@
         for i in range(4):
             b_local(i).start()
 
-    for k in range(4):
+    hail(0)
+
+    @pl.when(edge)
+    def _():
+        for i in range(16):
+            far_copy(i).start()
+
+    for k in range(1, 4):
         hail(k)
 
     @pl.when(edge)
@@ -163,15 +162,6 @@
     for i in range(2):
         a_local(i).wait()
     arrived(aa.at[pl.ds(0, 2)], r_a)
-
-    def forward(s, pieces):
-        @pl.when(jnp.logical_not(edge))
-        def _():
-            for at, k in pieces:
-                @pl.when(s == at)
-                def _():
-                    ps_copy(k).wait_recv()
-                    fw_copy(k).start()
 
     def core_copy(t):
         return send(give.at[t % 2], take.at[t], s_core.at[t % 2], r_core.at[t], dev(zh, x, y, 1 - core, c))
@@ -300,11 +290,8 @@
             f(t)
 
     def step(s, _):
-        forward(s, [(6, 12), (6, 13), (7, 14), (7, 15)])
         when(s < 8, multiply, s)
-        forward(s, [(k, 2 * k) for k in range(6)])
         when((s >= 1) & (s < 9), add_cores, s - 1)
-        forward(s, [(k, 2 * k + 1) for k in range(6)])
         when((s >= 3) & (s < 11), add_first, s - 3)
         when(s >= 5, add_second, s - 5)
         return 0
@@ -404,7 +391,6 @@
     @pl.when(jnp.logical_not(edge))
     def _():
         arrived(bb.at[pl.ds(0, 4)], s_b1)
-        arrived(bb.at[pl.ds(4, 4)], s_fw)
 
     core_copy(6).wait_send()
     core_copy(7).wait_send()
@@ -443,7 +429,6 @@
     buffers = [
         V((4, TOK, 512), bf16),
         V((8, TOK, WIDE), bf16),
-        V((4, TOK, WIDE), bf16),
         V((STEPS, 2, 4, 4, ROWS, 128), f32),
         V((2, 2, 4, 4, ROWS, 128), f32),
         V((STEPS, 2, 4, 4, ROWS, 128), f32),
@@ -458,7 +443,7 @@
         V((1, FEAT), f32), V((15, 1, FEAT), f32), V((1, FEAT), f32), V((3, 1, FEAT), f32),
         V((1, FEAT + 128), f32), V((15, 1, FEAT + 128), f32), V((8, 128), f32), V((15, 8, 128), f32),
     ]
-    sems = [S((6,)), S(()), S(()), S(()), S((4,)), S(()), S((4,)), S((16,)), S(()),
+    sems = [S((6,)), S(()), S(()), S(()), S((4,)), S(()), S((4,)),
             S((2,)), S((8,)), S((8,)), S((8,)), S((8,)), S((8,)), S(()), S((2,))] + [S(())] * 10 + [pltpu.SemaphoreType.REGULAR((4,))]
     shape = lambda *dims: jax.ShapeDtypeStruct(dims, f32)
     grad, by_row, by_col, nr, nc = pl.pallas_call(

time: 126 us -> 122 us (0.968)
  Pallas kernels: 125 us -> 121 us
    pallas_call x1, Pallas kernels: 123 us -> 119 us  [body(): pl.pallas_call(kernel, out_shape=[shape(ROWS, FEAT), shape(ROWS, 128), sh...]
where the time goes in v5:
time: 122 us
  Pallas kernels  121 us (99%)
    pallas_call x1, Pallas kernels, body(): pl.pallas_call(kernel, out_shape=[shape(ROWS, FEAT), shape(ROWS, 128), sh...  119 us

profile of v5, /device:TPU:1, one launch (start us, length us, event | category | flops | bytes accessed | tf_op | source)
XLA Modules:
  0.0 121.8 jit_solution(1399115440795807286)
XLA Ops:
  0.6 119.2 %shard_map.84 = (f32[64,1024]{1,0:T(8,128)}, f32[64,128]{1,0:T(8,128)}, f32[1,1024]{1,0:T(1,128)}, f32[1,64]{1,0:T(1,128)}, f32[1,1024]{1,0:T(1,128)}) custom-call(bf16[768,1024]{1,0:T(8,128)(2,1)} %a_ref.1, bf16[768,1024]{1,0:T(8,128)(2,1)} %b_ref.1, f32[1,64]{1,0:T(1,128)} %bitcast.5, f32[1,1024]{1,0:T(1,128)} %bitcast.4), custom_call_target="tpu_custom_call" | custom-call | tf_op jit(solution)/shard_map/pallas_call | solution.py:449
  119.9 1.9 %shard_map.85 = (f32[64,1024]{1,0:T(8,128)}, f32[64,1024]{1,0:T(8,128)}, f32[1,64]{1,0:T(1,128)}, f32[1,1024]{1,0:T(1,128)}) custom-call(f32[64,1024]{1,0:T(8,128)} %get-tuple-element.13.grad_ref, f32[64,128]{1,0:T(8,128)} %get-tuple-element.14.by_row_ref, f32[1,1024]{1,0:T(1,128)} %get-tuple-element.15.by_col_ref, f32[64,1024]{1,0:T(8,128)} %w_ref.1, ...), custom_call_target="tpu_custom_call" | custom-call | tf_op jit(solution)/shard_map/pallas_call | solution.py:459

commit v6 on v5

--- a/solution.py
+++ b/solution.py
@@ -15,9 +15,12 @@
 
 TOK = 768
 FEAT = 1024
-STEPS = 8
+CHUNKS = 8
 WIDE = 256
+NARROW = 128
+LAG1, LAG2 = 3, 5
 ROWS = 64
+HALF = 32
 
 
 POWER = 16
@@ -45,7 +48,7 @@
 def kernel(
     a_ref, b_ref, rm_ref, cm_ref,
     grad_out, by_row_ref, by_col_ref, nr_ref, nc_ref,
-    aa, bb, own, give, take, enc, in1, mid, in2, res, fin, grad,
+    aa, bb, bn, hown, hgive, htake, henc, hin1, hmid, hin2, own, give, take, enc, in1, mid, in2, whole, nres, res, fin, grad,
     row_in, col_mine, col_in, col_mid, col_in2, sca_mine, sca_in, sca_mid, sca_in2,
     s_loc, s_a, r_a, s_b1, r_b1, s_b2, r_b2,
     s_core, r_core, s_1, r_1, s_2, r_2, s_z, r_z, s_row, s_col, r_row, r_col, s_col2, r_col2, s_sca, r_sca, s_sca2, r_sca2, heard,
@@ -102,19 +105,19 @@
         return send(b_ref.at[:, pl.ds(WIDE * i, WIDE)], bb.at[i], s_b1, r_b1.at[i], to_mid)
 
     def piece(i):
-        return pl.ds(192 * (i % 4), 192)
+        return pl.ds(384 * (i % 2), 384)
 
     def b_piece(i):
-        return b_ref.at[piece(i), pl.ds(WIDE * (i // 4), WIDE)]
+        return b_ref.at[piece(i), pl.ds(NARROW * (i // 2), NARROW)]
 
     def bb_piece(i):
-        return bb.at[4 + i // 4, piece(i)]
+        return bn.at[i // 2, piece(i)]
 
     def b2_copy(i):
-        return send(b_piece(i), bb_piece(i), s_b2, r_b2.at[i // 4], to_pair)
+        return send(b_piece(i), bb_piece(i), s_b2, r_b2.at[i // 2], to_pair)
 
     def far_copy(i):
-        return send(b_piece(i), bb_piece(i), s_b2, r_b2.at[i // 4], dev(zh, x, y, core, jnp.where(c == 0, 2, 1)))
+        return send(b_piece(i), bb_piece(i), s_b2, r_b2.at[i // 2], dev(zh, x, y, core, jnp.where(c == 0, 2, 1)))
 
     @pl.when(edge)
     def _():
@@ -161,39 +164,124 @@
 
     for i in range(2):
         a_local(i).wait()
-    arrived(aa.at[pl.ds(0, 2)], r_a)
-
-    def core_copy(t):
-        return send(give.at[t % 2], take.at[t], s_core.at[t % 2], r_core.at[t], dev(zh, x, y, 1 - core, c))
-
-    def multiply(t):
-        @pl.when((t < 4) & jnp.logical_not(edge))
+
+    sibling = dev(zh, x, y, 1 - core, c)
+
+    def split(r, yy):
+        lo, hi = r[128 * yy : 128 * yy + 64], r[128 * yy + 64 : 128 * yy + 128]
+        return jnp.where(core == 0, lo, hi), jnp.where(core == 0, hi, lo)
+
+    def product(xx, b):
+        return lax.dot_general(aa[xx], b, (((0,), (0,)), ((), ())), preferred_element_type=jnp.float32)
+
+    def half_core(u):
+        return send(hgive.at[u % 2], htake.at[u], s_core.at[u % 2], r_core.at[u], sibling)
+
+    def half_rows(u):
+        return jnp.where(u < 4, half, 1 - half)
+
+    def half_multiply(u):
+        @pl.when(jnp.logical_not(edge))
         def _():
             for k in range(4):
-                @pl.when(t == k)
+                @pl.when(u == k)
                 def _():
                     b1_copy(k).wait_recv()
 
-        for k in range(4, 8):
-            @pl.when(t == k)
+        @pl.when(u == 4)
+        def _():
+            arrived(aa.at[pl.ds(0, 2)], r_a)
+
+        @pl.when(u >= 2)
+        def _():
+            half_core(u - 2).wait_send()
+
+        def of_x(k, _):
+            r = product(2 * half_rows(u) + k, bb[u % 4])
+            for yy in range(4):
+                keep, go = split(r, yy)
+                hown[u, yy, k] = keep
+                hgive[u % 2, yy, k] = go
+            return 0
+
+        lax.fori_loop(0, 2, of_x, 0)
+        half_core(u).start()
+
+    def half_copies_1(u):
+        return [
+            send(henc.at[u, lax.rem(y + j, 4)], hin1.at[u, j - 1], s_1.at[u], r_1.at[u],
+                 dev(zh, x, lax.rem(y + j, 4), core, c))
+            for j in range(1, 4)
+        ]
+
+    def half_add_cores(u):
+        half_core(u).wait_recv()
+
+        def of(q, _):
+            v = hown[u, q] + htake[u, q]
+
+            @pl.when(q == y)
             def _():
-                arrived(bb.at[k], r_b2.at[k - 4])
+                hown[u, q] = v
+
+            @pl.when(q != y)
+            def _():
+                code, scale = coded(v.reshape(2 * ROWS, WIDE))
+                henc[u, q, : 2 * ROWS] = code
+                henc[u, q, 2 * ROWS :] = scale
+
+            return 0
+
+        lax.fori_loop(0, 4, of, 0)
+        for q in half_copies_1(u):
+            q.start()
+
+    def half_copy_2(u, k):
+        to = 2 * half_rows(u) + k
+        j = lax.rem(to - x + 4, 4)
+        return send(hmid.at[u, k], hin2.at[u % 4, j - 1], s_2.at[u % 4], r_2.at[u % 4], dev(zh, to, y, core, c))
+
+    def half_add_first(u):
+        arrived(hin1.at[u], r_1.at[u])
+        total = hown[u, y].reshape(2 * ROWS, WIDE)
+        for k in range(3):
+            total = total + decoded(hin1[u, k, : 2 * ROWS], hin1[u, k, 2 * ROWS :])
+        hmid[u] = total.reshape(2, ROWS, WIDE)
+        for k in range(2):
+            @pl.when(x != 2 * half_rows(u) + k)
+            def _():
+                half_copy_2(u, k).start()
+
+    def half_add_second(u):
+        @pl.when(x // 2 == half_rows(u))
+        def _():
+            t = u % 4
+            arrived(hin2.at[t], r_2.at[t])
+            total = hmid[u, x % 2] + hin2[t, 0] + hin2[t, 1] + hin2[t, 2]
+            hand_over(t, total)
+
+    def core_copy(t):
+        return send(give.at[t % 2], take.at[t], s_core.at[t % 2], r_core.at[8 + t], sibling)
+
+    def multiply(t):
+        arrived(bn.at[t], r_b2.at[t])
+
+        @pl.when(t < 2)
+        def _():
+            half_core(6 + t).wait_send()
 
         @pl.when(t >= 2)
         def _():
             core_copy(t - 2).wait_send()
 
         def of_x(xx, _):
-            r = lax.dot_general(
-                aa[xx], bb[t], (((0,), (0,)), ((), ())), preferred_element_type=jnp.float32
-            )
+            r = product(xx, bn[t])
             for yy in range(4):
-                lo, hi = r[128 * yy : 128 * yy + 64], r[128 * yy + 64 : 128 * yy + 128]
-                keep, go = jnp.where(core == 0, lo, hi), jnp.where(core == 0, hi, lo)
-                own[t, 0, xx, yy] = keep[:, :128]
-                own[t, 1, yy, xx] = keep[:, 128:]
-                give[t % 2, 0, xx, yy] = go[:, :128]
-                give[t % 2, 1, yy, xx] = go[:, 128:]
+                keep, go = split(r, yy)
+                own[t, 0, xx, yy] = keep[:HALF]
+                own[t, 1, yy, xx] = keep[HALF:]
+                give[t % 2, 0, xx, yy] = go[:HALF]
+                give[t % 2, 1, yy, xx] = go[HALF:]
             return 0
 
         lax.fori_loop(0, 4, of_x, 0)
@@ -202,9 +290,9 @@
     def copies_1(t):
         out = []
         for j in range(1, 4):
-            out.append(send(enc.at[t, 0, lax.rem(x + j, 4)], in1.at[t, 0, j - 1], s_1.at[t], r_1.at[t],
+            out.append(send(enc.at[t, 0, lax.rem(x + j, 4)], in1.at[t, 0, j - 1], s_1.at[8 + t], r_1.at[8 + t],
                             dev(zh, lax.rem(x + j, 4), y, core, c)))
-            out.append(send(enc.at[t, 1, lax.rem(y + j, 4)], in1.at[t, 1, j - 1], s_1.at[t], r_1.at[t],
+            out.append(send(enc.at[t, 1, lax.rem(y + j, 4)], in1.at[t, 1, j - 1], s_1.at[8 + t], r_1.at[8 + t],
                             dev(zh, x, lax.rem(y + j, 4), core, c)))
         return out
 
@@ -222,9 +310,9 @@
 
             @pl.when(jnp.logical_not(mine))
             def _():
-                code, scale = coded(v.reshape(4 * ROWS, 128))
-                enc[t, h, q, : 4 * ROWS] = code
-                enc[t, h, q, 4 * ROWS :] = scale
+                code, scale = coded(v.reshape(4 * HALF, 128))
+                enc[t, h, q, : 4 * HALF] = code
+                enc[t, h, q, 4 * HALF :] = scale
 
             return 0
 
@@ -235,18 +323,18 @@
     def copies_2(t):
         out = []
         for j in range(1, 4):
-            out.append(send(mid.at[t, 0, lax.rem(y + j, 4)], in2.at[t, 0, j - 1], s_2.at[t], r_2.at[t], dev(zh, x, lax.rem(y + j, 4), core, c)))
-            out.append(send(mid.at[t, 1, lax.rem(x + j, 4)], in2.at[t, 1, j - 1], s_2.at[t], r_2.at[t], dev(zh, lax.rem(x + j, 4), y, core, c)))
+            out.append(send(mid.at[t, 0, lax.rem(y + j, 4)], in2.at[t, 0, j - 1], s_2.at[4 + t], r_2.at[4 + t], dev(zh, x, lax.rem(y + j, 4), core, c)))
+            out.append(send(mid.at[t, 1, lax.rem(x + j, 4)], in2.at[t, 1, j - 1], s_2.at[4 + t], r_2.at[4 + t], dev(zh, lax.rem(x + j, 4), y, core, c)))
         return out
 
     def add_first(t):
-        arrived(in1.at[t], r_1.at[t])
+        arrived(in1.at[t], r_1.at[8 + t])
 
         def of(h, _):
-            total = own[t, h, jnp.where(h == 0, x, y)].reshape(4 * ROWS, 128)
+            total = own[t, h, jnp.where(h == 0, x, y)].reshape(4 * HALF, 128)
             for k in range(3):
-                total = total + decoded(in1[t, h, k, : 4 * ROWS], in1[t, h, k, 4 * ROWS :])
-            mid[t, h] = total.reshape(4, ROWS, 128)
+                total = total + decoded(in1[t, h, k, : 4 * HALF], in1[t, h, k, 4 * HALF :])
+            mid[t, h] = total.reshape(4, HALF, 128)
             return 0
 
         lax.fori_loop(0, 2, of, 0)
@@ -263,26 +351,33 @@
         return send(res.at[t], fin.at[zh, lax.rem(t, 4)], s_z, r_z.at[zh],
                     dev(c // 2, x, y, core, target(t)))
 
+    def hand_over(t, total):
+        code, scale = coded(total)
+
+        @pl.when(stays(t))
+        def _():
+            fin[zh, t, :ROWS] = code
+            fin[zh, t, ROWS:] = scale
+
+        @pl.when(jnp.logical_not(stays(t)))
+        def _():
+            res[t, :ROWS] = code
+            res[t, ROWS:] = scale
+            z_copy(t).start()
+
+    def narrow_copy(t):
+        return send(nres.at[t], fin.at[zh, t // 2, :, pl.ds(pl.multiple_of(NARROW * (t % 2), NARROW), NARROW)], s_z, r_z.at[zh],
+                    dev(c // 2, x, y, core, target(4)))
+
     def add_second(t):
-        arrived(in2.at[t], r_2.at[t])
-        lo = mid[t, 0, y] + in2[t, 0, 0] + in2[t, 0, 1] + in2[t, 0, 2]
-        hi = mid[t, 1, x] + in2[t, 1, 0] + in2[t, 1, 1] + in2[t, 1, 2]
-        (lo, lo_scale), (hi, hi_scale) = coded(lo), coded(hi)
-
-        def put(ref):
-            ref[:ROWS, :128] = lo
-            ref[:ROWS, 128:] = hi
-            ref[ROWS:, :128] = lo_scale
-            ref[ROWS:, 128:] = hi_scale
-
-        @pl.when(stays(t))
-        def _():
-            put(fin.at[zh, lax.rem(t, 4)])
-
-        @pl.when(jnp.logical_not(stays(t)))
-        def _():
-            put(res.at[t])
-            z_copy(t).start()
+        arrived(in2.at[t], r_2.at[4 + t])
+        for h in range(2):
+            at = pl.ds(HALF * h, HALF)
+            whole[at] = mid[t, h, y if h == 0 else x] + in2[t, h, 0] + in2[t, h, 1] + in2[t, h, 2]
+        code, scale = coded(whole[...])
+        nres[t, :ROWS] = code
+        nres[t, ROWS:] = scale
+        narrow_copy(t).start()
 
     def when(cond, f, t):
         @pl.when(cond)
@@ -290,13 +385,20 @@
             f(t)
 
     def step(s, _):
-        when(s < 8, multiply, s)
-        when((s >= 1) & (s < 9), add_cores, s - 1)
-        when((s >= 3) & (s < 11), add_first, s - 3)
-        when(s >= 5, add_second, s - 5)
+        when(s < 8, half_multiply, s)
+        when((s >= 8) & (s < 16), multiply, s - 8)
+        u = s - 1
+        when((u >= 0) & (u < 8), half_add_cores, u)
+        when((u >= 8) & (u < 16), add_cores, u - 8)
+        u = s - LAG1
+        when((u >= 0) & (u < 8), half_add_first, u)
+        when((u >= 8) & (u < 16), add_first, u - 8)
+        u = s - LAG2
+        when((u >= 0) & (u < 8), half_add_second, u)
+        when(u >= 8, add_second, u - 8)
         return 0
 
-    lax.fori_loop(0, 13, step, 0)
+    lax.fori_loop(0, 16 + LAG2, step, 0)
 
     source = 2 * zh + c // 2
     for g in range(2):
@@ -386,22 +488,28 @@
 
     grad_copy.wait()
     arrived(aa.at[pl.ds(0, 2)], s_a)
-    arrived(bb.at[pl.ds(4, 4)], s_b2)
+    arrived(bn, s_b2)
 
     @pl.when(jnp.logical_not(edge))
     def _():
-        arrived(bb.at[pl.ds(0, 4)], s_b1)
+        arrived(bb, s_b1)
 
     core_copy(6).wait_send()
     core_copy(7).wait_send()
 
     def sent(t):
-        arrived(in1.at[t], s_1.at[t])
-        arrived(in2.at[t], s_2.at[t])
-
-        @pl.when(jnp.logical_not(stays(t)))
-        def _():
-            z_copy(t).wait_send()
+        arrived(hin1.at[t], s_1.at[t])
+        arrived(in1.at[t], s_1.at[8 + t])
+        arrived(in2.at[t], s_2.at[4 + t])
+        narrow_copy(t).wait_send()
+
+        @pl.when(t < 4)
+        def _():
+            arrived(hin2.at[t], s_2.at[t])
+
+            @pl.when(jnp.logical_not(stays(t)))
+            def _():
+                z_copy(t).wait_send()
 
     each(0, 8, sent)
     arrived(row_in.at[pl.ds(1, 3)], s_row)
@@ -428,23 +536,33 @@
     vmem, hbm = pl.BlockSpec(memory_space=pltpu.VMEM), pl.BlockSpec(memory_space=pl.ANY)
     buffers = [
         V((4, TOK, 512), bf16),
-        V((8, TOK, WIDE), bf16),
-        V((STEPS, 2, 4, 4, ROWS, 128), f32),
-        V((2, 2, 4, 4, ROWS, 128), f32),
-        V((STEPS, 2, 4, 4, ROWS, 128), f32),
-        V((STEPS, 2, 4, 4 * ROWS + 16, 128), bf16),
-        V((STEPS, 2, 3, 4 * ROWS + 16, 128), bf16),
-        V((STEPS, 2, 4, ROWS, 128), f32),
-        V((STEPS, 2, 3, ROWS, 128), f32),
-        V((STEPS, ROWS + 16, WIDE), bf16),
+        V((4, TOK, WIDE), bf16),
+        V((CHUNKS, TOK, NARROW), bf16),
+        V((8, 4, 2, ROWS, WIDE), f32),
+        V((2, 4, 2, ROWS, WIDE), f32),
+        V((8, 4, 2, ROWS, WIDE), f32),
+        V((8, 4, 2 * ROWS + 16, WIDE), bf16),
+        V((8, 3, 2 * ROWS + 16, WIDE), bf16),
+        V((8, 2, ROWS, WIDE), f32),
+        V((4, 3, ROWS, WIDE), f32),
+        V((CHUNKS, 2, 4, 4, HALF, 128), f32),
+        V((2, 2, 4, 4, HALF, 128), f32),
+        V((CHUNKS, 2, 4, 4, HALF, 128), f32),
+        V((CHUNKS, 2, 4, 4 * HALF + 16, 128), bf16),
+        V((CHUNKS, 2, 3, 4 * HALF + 16, 128), bf16),
+        V((CHUNKS, 2, 4, HALF, 128), f32),
+        V((CHUNKS, 2, 3, HALF, 128), f32),
+        V((ROWS, NARROW), f32),
+        V((CHUNKS, ROWS + 16, NARROW), bf16),
+        V((4, ROWS + 16, WIDE), bf16),
         V((2, 4, ROWS + 16, WIDE), bf16),
         V((ROWS, FEAT), f32),
         V((4, ROWS, 128), f32),
         V((1, FEAT), f32), V((15, 1, FEAT), f32), V((1, FEAT), f32), V((3, 1, FEAT), f32),
         V((1, FEAT + 128), f32), V((15, 1, FEAT + 128), f32), V((8, 128), f32), V((15, 8, 128), f32),
     ]
-    sems = [S((6,)), S(()), S(()), S(()), S((4,)), S(()), S((4,)),
-            S((2,)), S((8,)), S((8,)), S((8,)), S((8,)), S((8,)), S(()), S((2,))] + [S(())] * 10 + [pltpu.SemaphoreType.REGULAR((4,))]
+    sems = [S((6,)), S(()), S(()), S(()), S((4,)), S(()), S((8,)),
+            S((2,)), S((16,)), S((16,)), S((16,)), S((12,)), S((12,)), S(()), S((2,))] + [S(())] * 10 + [pltpu.SemaphoreType.REGULAR((4,))]
     shape = lambda *dims: jax.ShapeDtypeStruct(dims, f32)
     grad, by_row, by_col, nr, nc = pl.pallas_call(
         kernel,

time: 122 us -> 121 us (level)
    pallas_call x1, Pallas kernels: 119 us -> 118 us  [body(): pl.pallas_call(kernel, out_shape=[shape(ROWS, FEAT), shape(ROWS, 128), sh...]
where the time goes in v6:
time: 121 us; the launch traced here: 120 us
  Pallas kernels  120 us (99%)
    pallas_call x1, Pallas kernels, body(): pl.pallas_call(kernel, out_shape=[shape(ROWS, FEAT), shape(ROWS, 128), sh...  118 us

profile of v6, /device:TPU:1, one launch (start us, length us, event | category | flops | bytes accessed | tf_op | source)
XLA Modules:
  0.0 120.5 jit_solution(16768363815612712062)
XLA Ops:
  0.6 117.9 %shard_map.84 = (f32[64,1024]{1,0:T(8,128)}, f32[64,128]{1,0:T(8,128)}, f32[1,1024]{1,0:T(1,128)}, f32[1,64]{1,0:T(1,128)}, f32[1,1024]{1,0:T(1,128)}) custom-call(bf16[768,1024]{1,0:T(8,128)(2,1)} %a_ref.1, bf16[768,1024]{1,0:T(8,128)(2,1)} %b_ref.1, f32[1,64]{1,0:T(1,128)} %bitcast.5, f32[1,1024]{1,0:T(1,128)} %bitcast.4), custom_call_target="tpu_custom_call" | custom-call | tf_op jit(solution)/shard_map/pallas_call | solution.py:567
  118.5 1.9 %shard_map.85 = (f32[64,1024]{1,0:T(8,128)}, f32[64,1024]{1,0:T(8,128)}, f32[1,64]{1,0:T(1,128)}, f32[1,1024]{1,0:T(1,128)}) custom-call(f32[64,1024]{1,0:T(8,128)} %get-tuple-element.13.grad_ref, f32[64,128]{1,0:T(8,128)} %get-tuple-element.14.by_row_ref, f32[1,1024]{1,0:T(1,128)} %get-tuple-element.15.by_col_ref, f32[64,1024]{1,0:T(8,128)} %w_ref.1, ...), custom_call_target="tpu_custom_call" | custom-call | tf_op jit(solution)/shard_map/pallas_call | solution.py:577
